TPU v7x, 256 devices: a whole 4x4x8 slice. The times are simulated.
256 devices in a mesh: slab: 16 (over y, x), ex: 16 (over z, core).
Axes of the slice: x: 4, y: 4, z: 8, core: 2. Of those that a mesh axis runs over, the one named last changes fastest.
Arguments:
- hidden: bfloat16 [8192, 28672], P('ex', 'slab'), may hold values from -6 to 6
- out_grad: bfloat16 [8192, 8192], P('ex', 'slab'), may hold values from -6 to 6
- lengths: int32 [64], P('ex'), may hold values from 16 to 128
- left_signs: bfloat16 [224, 2, 16, 128], P('slab'), may hold values from -1 to 1, as said below
- left_index: int32 [224, 2], P('slab'), may hold values from 0 to 3, as said below
- right_signs: bfloat16 [128, 8192], P(None, 'slab'), may hold values from -1 to 1, as said below
Outputs:
- gram: float32 [8192, 8192], P('slab', 'ex')
Inputs may be any that keep to these rules, and one draw needn't show every extreme that they name: `left_index`: the 2 column blocks listed for one row block differ. `left_signs`: every entry is +1 or -1. `right_signs`: every entry is +1 or -1.
All inputs are finite; a program needn't handle non-finite values.
Results may differ from a plain program's by a relative error of at most 0.0003.
Values sent between devices are 32-bit elements; how exact they have to be, the bound alone decides.
A program may use at most 64 MiB of HBM per device.

v0:
```python
import jax
import jax.numpy as jnp
from jax import lax
from jax.sharding import PartitionSpec as P

D = 8192
FF = 28672
SEQ = 128
BF = 128
KB = 4
BK = 16
K2 = 128
K1 = 64


def build_left(left_signs, left_index):
    onehot = (left_index[:, :, None] == jnp.arange(KB, dtype=jnp.int32)[None, None, :]).astype(
        jnp.bfloat16
    )
    dense = jnp.einsum("rnc,rnkf->rfck", onehot, left_signs, preferred_element_type=jnp.float32)
    return dense.reshape(left_signs.shape[0] * BF, KB * BK).astype(jnp.bfloat16)


def features_of(act_part, grad_part):
    outer = jnp.einsum("etk,etl->ekl", act_part, grad_part, precision=lax.Precision.HIGHEST)
    return outer.reshape(outer.shape[0], -1) * SEQ ** (-0.5)


def shards(hidden, out_grad, lengths, left_signs, left_index, right_signs):
    ex_dev = lengths.shape[0]
    examples = ex_dev * lax.axis_size("ex")
    positions = lax.broadcasted_iota(jnp.int32, (ex_dev, SEQ), 1)
    keep = (positions < lengths[:, None]).reshape(-1, 1)
    masked = jnp.where(keep, hidden, jnp.zeros_like(hidden))
    left = build_left(left_signs, left_index)
    act_part = jnp.dot(masked, left, preferred_element_type=jnp.float32) * FF ** (-0.5)
    grad_part = lax.dot_general(
        out_grad, right_signs, (((1,), (1,)), ((), ())), preferred_element_type=jnp.float32
    ) * D ** (-0.5)
    act_proj, grad_proj = lax.psum((act_part, grad_part), "slab")
    act_proj = act_proj.reshape(ex_dev, SEQ, K1)
    grad_proj = grad_proj.reshape(ex_dev, SEQ, K2)
    row_width = K1 // lax.axis_size("slab")
    row_start = lax.axis_index("slab") * row_width
    act_rows = lax.dynamic_slice_in_dim(act_proj, row_start, row_width, 2)
    row_feats = features_of(act_rows, grad_proj)
    col_feats = features_of(act_proj, grad_proj)
    summed = lax.psum_scatter(
        jnp.dot(col_feats.T, row_feats, precision=lax.Precision.HIGHEST),
        "ex",
        scatter_dimension=0,
        tiled=True,
    )
    return summed.T / examples


def solution(mesh):
    in_specs = (
        P("ex", "slab"),
        P("ex", "slab"),
        P("ex"),
        P("slab", None, None, None),
        P("slab", None),
        P(None, "slab"),
    )
    out_specs = P("slab", "ex")
    return jax.shard_map(shards, mesh=mesh, in_specs=in_specs, out_specs=out_specs, check_vma=False)
```

profile of v0, /device:TPU:1, one launch (start us, length us, event | category | flops | bytes accessed | tf_op | source)
XLA Modules:
  0.0 239.2 jit_solution(4063031139104457222)
XLA Ops:
  6.5 0.0 copy-start
  6.5 0.0 all-reduce.3.cloned.1.call-start
  6.5 0.8 fusion.26
  7.3 0.8 copy.11
  8.1 1.3 fusion.3
  9.4 0.2 copy.13
  9.6 0.0 copy-start.1
  9.6 2.3 fusion.7
  11.9 0.7 copy.36
  12.6 0.0 copy-done
  12.6 0.0 copy-done.1
  12.6 1.0 convolution_multiply_fusion
  13.6 0.0 all-reduce.3.cloned.1.call-update
  13.6 0.0 reduce-scatter.2.cloned.1.call-start
  13.7 97.1 %all-reduce.3.cloned.1.call-done = (f32[4,128,64]{1,2,0:T(8,128)}, f32[4,128,128]{2,1,0:T(8,128)}) async-done(((f32[4,128,64]{1,2,0:T(8,128)}, f32[4,128,128]{2,1,0:T(8,128)}), (f32[4,128,64]{1,2,0:T(8,128)}, f32[4,128,128]{2,1,0:T(8,128)})) %all-reduce.3.cloned.1.call-update) | async-done | bytes 393232 | tf_op jit(solution)/shard_map/psum | solution.py:40
  110.7 1.4 fusion.10
  112.1 1.3 fusion.11
  113.4 15.9 %fusion.15 = f32[8192,512]{1,0:T(8,128)} fusion(f32[1,4,64,128]{3,2,1,0:T(8,128)S(1)} %fusion.10, f32[1,4,4,128]{3,2,1,0:T(4,128)S(1)} %fusion.11), kind=kOutput, calls=%fused_computation.16 | convolution fusion | flops 201326592 | bytes 16916480 | tf_op jit(solution)/shard_map/dot_general | solution.py:49
  129.3 0.0 reduce-scatter.2.cloned.1.call-update
  129.4 100.3 %reduce-scatter.2.cloned.1.call-done = f32[512,512]{1,0:T(8,128)} async-done(((f32[8192,512]{1,0:T(8,128)}), f32[512,512]{1,0:T(8,128)}) %reduce-scatter.2.cloned.1.call-update) | async-done | bytes 1048592 | tf_op jit(solution)/shard_map/reduce_scatter | solution.py:48
  229.7 1.3 multiply_bitcast_fusion
  231.0 1.3 copy.15
Async XLA Ops:
  6.5 6.0 %copy-start = (bf16[512,512]{1,0:T(8,128)(2,1)S(1)}, bf16[512,512]{1,0:T(8,128)(2,1)}, u32[]{:S(2)}) copy-start(bf16[512,512]{1,0:T(8,128)(2,1)} %param.7) | copy-start | bytes 1572868
  6.5 104.2 %all-reduce.3.cloned.1.call-start = ((), (), s32[]{:S(2)}) async-start(), calls=%async_computation.2 | async-start | bytes 786432 | tf_op jit(solution)/shard_map/psum | solution.py:40
  9.6 3.0 %copy-start.1 = (bf16[128,512]{1,0:T(8,128)(2,1)S(1)}, bf16[128,512]{1,0:T(8,128)(2,1)}, u32[]{:S(2)}) copy-start(bf16[128,512]{1,0:T(8,128)(2,1)} %param.11) | copy-start | bytes 393220
  13.6 216.1 %reduce-scatter.2.cloned.1.call-start = ((), (), s32[]{:S(2)}) async-start(), calls=%async_computation.1 | async-start | bytes 17825792 | tf_op jit(solution)/shard_map/reduce_scatter | solution.py:48
Sparse Core Ops, SparseCore 0:
  13.7 96.9 all-reduce.2
  129.5 100.1 reduce-scatter.1
where the time goes:
time: 240 us; the launch traced here: 239 us
  waiting for transfers between devices  197 us (82%)
  matrix products  23.2 us (10%)
  between operations  13.4 us (6%)
  local copies, waits for them, and re-layouts  2.92 us (1%)
    reduce_scatter x1, waiting for transfers between devices, shards(): lax.psum_scatter(jnp.dot(col_feats.T, row_feats, precision=lax.Precision....  100 us
    psum x1, waiting for transfers between devices, shards(): act_proj, grad_proj = lax.psum((act_part, grad_part), 'slab')  97.1 us
    dot_general x1, matrix products, shards(): jnp.dot(col_feats.T, row_feats, precision=lax.Precision.HIGHEST)  15.9 us
  transfers between devices with their start and end apart: 2, of which 2 were waited for; matrix products, arithmetic and copies ran while one was open for 0% of the time, Pallas kernels for 0%

commit v1 on v0

v1 whole, which is shorter than its diff:
```python
import functools

import jax
import jax.numpy as jnp
from jax import lax
from jax.experimental import pallas as pl
from jax.experimental.pallas import tpu as pltpu
from jax.sharding import PartitionSpec as P

D = 8192
FF = 28672
SEQ = 128
BF = 128
KB = 4
BK = 16
K2 = 128
K1 = 64
EX_DEV = 4
PEERS = 16
ZS = 8
TOK = SEQ // EX_DEV
HALF = TOK // 2
CHUNK = TOK + HALF

MESH = pl.DeviceIdType.MESH
F32 = jnp.float32
BF16 = jnp.bfloat16
NT = (((1,), (1,)), ((), ()))
TN = (((0,), (0,)), ((), ()))


def split(x):
    high = x.astype(BF16)
    return high, (x - high.astype(F32)).astype(BF16)


def remote(src, dst, send_sem, recv_sem, slab, ex):
    return pltpu.make_async_remote_copy(
        src_ref=src,
        dst_ref=dst,
        send_sem=send_sem,
        recv_sem=recv_sem,
        device_id=(slab, ex),
        device_id_type=MESH,
    )


def wait_bytes(ref, sem):
    pltpu.make_async_copy(ref, ref, sem).wait()


def exchange(
    rows_per_block,
    hidden,
    out_grad,
    right,
    signs,
    index,
    lengths,
    a_out,
    b_out,
    hid_v,
    og_v,
    right_v,
    signs_v,
    left_v,
    part,
    part_in,
    feat,
    row_send,
    row_recv,
    col_send,
    col_recv,
    g_send,
    c_part,
    c_buf,
    r_buf,
    hid_sem,
    og_sem,
    par_sem,
    send_sem,
    recv_sem,
):
    s = lax.axis_index("slab")
    e = lax.axis_index("ex")
    y, x = s // EX_DEV, s % EX_DEV
    z, c = e // 2, e % 2
    place = c * ZS + z

    barrier = pltpu.get_barrier_semaphore()

    @pl.loop(1, PEERS)
    def _(i):
        pl.semaphore_signal(
            barrier, inc=1, device_id=(lax.rem(s + i, PEERS), e), device_id_type=MESH
        )
        pl.semaphore_signal(
            barrier, inc=1, device_id=(s, lax.rem(e + i, PEERS)), device_id_type=MESH
        )

    copies = []
    par = [
        pltpu.make_async_copy(signs, signs_v, par_sem.at[0]),
        pltpu.make_async_copy(right, right_v, par_sem.at[1]),
    ]
    for copy in par:
        copy.start()
    owners = [lax.rem(y + 1 + i, EX_DEV) for i in range(EX_DEV)]
    for i, j in enumerate(owners):
        rows = pl.ds(pl.multiple_of(j * SEQ, SEQ), SEQ)
        pair = (
            pltpu.make_async_copy(hidden.at[rows], hid_v.at[i], hid_sem.at[i]),
            pltpu.make_async_copy(out_grad.at[rows], og_v.at[i], og_sem.at[i]),
        )
        for copy in pair:
            copy.start()
        copies.append(pair)

    par[0].wait()
    for r in range(rows_per_block):
        blocks = [signs_v[r, n].astype(F32) for n in range(2)]
        for k in range(KB):
            on = [(index[r, n] == k).astype(F32) for n in range(2)]
            dense = (blocks[0] * on[0] + blocks[1] * on[1]).astype(BF16)
            cols = pl.ds(r * BF, BF)
            left_v[pl.ds(k * BK, BK), cols] = dense
            left_v[pl.ds(K1 + k * BK, BK), cols] = dense
    par[1].wait()

    lane = lax.broadcasted_iota(jnp.int32, (HALF, SEQ), 1)
    first = lane < K1
    token = lax.broadcasted_iota(jnp.int32, (SEQ, SEQ), 0)
    for i, j in enumerate(owners):
        for copy in copies[i]:
            copy.wait()
        act = lax.dot_general(hid_v[i], left_v[...], NT, preferred_element_type=F32)
        act = jnp.where(token < lengths[j], act, 0.0)
        grad = lax.dot_general(og_v[i], right_v[...], NT, preferred_element_type=F32)
        for q in range(EX_DEV):
            at = i * EX_DEV + q
            part[at, :TOK] = grad[q * TOK : (q + 1) * TOK]
            part[at, TOK:] = jnp.where(
                first,
                act[q * TOK : q * TOK + HALF],
                act[q * TOK + HALF : (q + 1) * TOK],
            )
        if i == 0:
            pl.semaphore_wait(barrier, 2 * (PEERS - 1))
        if i < EX_DEV - 1:
            for q in range(EX_DEV):
                remote(
                    part.at[i * EX_DEV + q],
                    part_in.at[s],
                    send_sem.at[0],
                    recv_sem.at[0],
                    j * EX_DEV + q,
                    e,
                ).start()
        else:
            for k in range(1, EX_DEV):
                q = lax.rem(x + k, EX_DEV)
                remote(
                    part.at[i * EX_DEV + q],
                    part_in.at[s],
                    send_sem.at[0],
                    recv_sem.at[0],
                    y * EX_DEV + q,
                    e,
                ).start()
    part_in[s] = part[(EX_DEV - 1) * EX_DEV + x]
    wait_bytes(part_in.at[pl.ds(0, PEERS - 1)], recv_sem.at[0])

    total = part_in[0]
    for i in range(1, PEERS):
        total += part_in[i]
    grad_h, grad_l = split(total[:TOK] * (D**-0.5 * SEQ**-0.5))
    packed = total[TOK:] * FF**-0.5
    acts = jnp.concatenate([jnp.where(first, packed, 0.0), jnp.where(first, 0.0, packed)], axis=0)
    act_h, act_l = split(acts)
    outer = lax.dot_general(
        jnp.concatenate([act_h, act_h, act_l, act_l], axis=0),
        jnp.concatenate([grad_h, grad_l, grad_h, grad_l], axis=0),
        TN,
        preferred_element_type=F32,
    )
    features = outer[:K1] + outer[K1:]
    feat[...] = features
    for i in range(PEERS):
        row_send[i] = features[i * EX_DEV : (i + 1) * EX_DEV]
    for m in range(EX_DEV):
        col_send[m] = feat[pl.ds(m, PEERS, stride=EX_DEV), :]

    for k in range(1, EX_DEV):
        q = lax.rem(x + k, EX_DEV)
        remote(
            col_send.at[q],
            col_recv.at[x],
            send_sem.at[1],
            recv_sem.at[1],
            y * EX_DEV + q,
            e,
        ).start()

    @pl.loop(1, PEERS)
    def _(i):
        to = lax.rem(s + i, PEERS)
        remote(row_send.at[to], row_recv.at[s], send_sem.at[2], recv_sem.at[2], to, e).start()

    col_recv[x] = col_send[x]
    row_recv[s] = row_send[s]
    wait_bytes(col_recv.at[pl.ds(0, EX_DEV - 1)], recv_sem.at[1])
    mine = col_recv[0] + col_recv[1] + col_recv[2] + col_recv[3]
    for i in range(PEERS):
        g_send[i] = mine[i : i + 1]

    @pl.loop(1, PEERS)
    def _(i):
        to = lax.rem(e + i, PEERS)
        remote(g_send.at[to], c_part.at[place], send_sem.at[3], recv_sem.at[3], s, to).start()

    c_part[place] = g_send[e]

    wait_bytes(row_recv.at[pl.ds(0, PEERS - 1)], recv_sem.at[2])
    rows = [
        row_recv[4 * j] + row_recv[4 * j + 1] + row_recv[4 * j + 2] + row_recv[4 * j + 3]
        for j in range(EX_DEV)
    ]
    own = pl.ds(pl.multiple_of(place * PEERS, PEERS), PEERS)
    r_buf[own] = jnp.concatenate(rows, axis=0)
    for k in range(1, ZS):
        to = lax.rem(z + k, ZS) * 2 + c
        remote(r_buf.at[own], r_buf.at[own], send_sem.at[4], recv_sem.at[4], s, to).start()

    wait_bytes(c_part.at[pl.ds(0, PEERS - 1)], recv_sem.at[3])
    c_buf[s] = c_part[...].reshape(PEERS, K2)

    @pl.loop(1, PEERS)
    def _(i):
        to = lax.rem(s + i, PEERS)
        remote(c_buf.at[s], c_buf.at[s], send_sem.at[5], recv_sem.at[5], to, e).start()

    seven = pl.ds(0, (ZS - 1) * PEERS)
    wait_bytes(r_buf.at[seven], recv_sem.at[4])
    side = pl.ds(pl.multiple_of(c * (ZS * PEERS), ZS * PEERS), ZS * PEERS)
    across = remote(
        r_buf.at[side], r_buf.at[side], send_sem.at[6], recv_sem.at[6], s, z * 2 + 1 - c
    )
    across.start()

    wait_bytes(c_buf.at[pl.ds(0, PEERS - 1)], recv_sem.at[5])
    cols = jnp.concatenate(
        [
            jnp.concatenate([c_buf[4 * j + m] for j in range(EX_DEV)], axis=0)
            for m in range(EX_DEV)
        ],
        axis=1,
    )
    high, low = split(cols)
    for k, piece in enumerate((high, low, high, low)):
        b_out[pl.ds(k * K1, K1)] = piece

    wait_bytes(r_buf.at[pl.ds(0, ZS * PEERS)], recv_sem.at[6])
    rows = jnp.concatenate(
        [
            jnp.concatenate(
                [r_buf[pl.ds(4 * j + m, PEERS, stride=PEERS), :] for j in range(EX_DEV)], axis=0
            )
            for m in range(EX_DEV)
        ],
        axis=1,
    )
    high, low = split(rows)
    for k, piece in enumerate((high, high, low, low)):
        a_out[pl.ds(k * K1, K1)] = piece

    wait_bytes(part.at[pl.ds(0, PEERS - 1)], send_sem.at[0])
    wait_bytes(col_send.at[pl.ds(0, EX_DEV - 1)], send_sem.at[1])
    wait_bytes(row_send.at[pl.ds(0, PEERS - 1)], send_sem.at[2])
    wait_bytes(g_send.at[pl.ds(0, PEERS - 1)], send_sem.at[3])
    wait_bytes(r_buf.at[seven], send_sem.at[4])
    wait_bytes(c_buf.at[pl.ds(0, PEERS - 1)], send_sem.at[5])
    wait_bytes(r_buf.at[pl.ds(0, ZS * PEERS)], send_sem.at[6])


def gram_block(a_ref, b_ref, out_ref):
    out_ref[...] = lax.dot_general(
        a_ref[...], b_ref[...], TN, preferred_element_type=F32
    ) * (1.0 / (PEERS * EX_DEV))


def shards(hidden, out_grad, lengths, left_signs, left_index, right_signs):
    tokens, ff = hidden.shape
    features = out_grad.shape[1]
    blocks = left_signs.shape[0]
    hbm = pl.BlockSpec(memory_space=pl.ANY)
    smem = pl.BlockSpec(memory_space=pltpu.SMEM)
    vmem = pl.BlockSpec(memory_space=pltpu.VMEM)
    wide = EX_DEV * K2
    a, b = pl.pallas_call(
        functools.partial(exchange, blocks),
        out_shape=[jax.ShapeDtypeStruct((EX_DEV * K1, wide), BF16)] * 2,
        in_specs=[hbm, hbm, hbm, hbm, smem, smem],
        out_specs=[vmem, vmem],
        scratch_shapes=[
            pltpu.VMEM((EX_DEV, SEQ, ff), BF16),
            pltpu.VMEM((EX_DEV, SEQ, features), BF16),
            pltpu.VMEM((K2, features), BF16),
            pltpu.VMEM((blocks, 2, BK, BF), BF16),
            pltpu.VMEM((2 * K1, ff), BF16),
            pltpu.VMEM((PEERS, CHUNK, SEQ), F32),
            pltpu.VMEM((PEERS, CHUNK, SEQ), F32),
            pltpu.VMEM((K1, K2), F32),
            pltpu.VMEM((PEERS, EX_DEV, K2), F32),
            pltpu.VMEM((PEERS, EX_DEV, K2), F32),
            pltpu.VMEM((EX_DEV, PEERS, K2), F32),
            pltpu.VMEM((EX_DEV, PEERS, K2), F32),
            pltpu.VMEM((PEERS, 1, K2), F32),
            pltpu.VMEM((PEERS, 1, K2), F32),
            pltpu.VMEM((PEERS, PEERS, K2), F32),
            pltpu.VMEM((PEERS * PEERS, K2), F32),
            pltpu.SemaphoreType.DMA((EX_DEV,)),
            pltpu.SemaphoreType.DMA((EX_DEV,)),
            pltpu.SemaphoreType.DMA((2,)),
            pltpu.SemaphoreType.DMA((7,)),
            pltpu.SemaphoreType.DMA((7,)),
        ],
        compiler_params=pltpu.CompilerParams(
            collective_id=0, has_side_effects=True, vmem_limit_bytes=32 * 1024 * 1024
        ),
        name="exchange",
    )(hidden, out_grad, right_signs, left_signs, left_index, lengths)
    return pl.pallas_call(
        gram_block,
        out_shape=jax.ShapeDtypeStruct((wide, wide), F32),
        in_specs=[vmem, vmem],
        out_specs=vmem,
        name="gram",
    )(a, b)


def solution(mesh):
    in_specs = (
        P("ex", "slab"),
        P("ex", "slab"),
        P("ex"),
        P("slab", None, None, None),
        P("slab", None),
        P(None, "slab"),
    )
    out_specs = P("slab", "ex")
    return jax.shard_map(shards, mesh=mesh, in_specs=in_specs, out_specs=out_specs, check_vma=False)
```

time: 240 us -> 40.4 us (0.17)
  waiting for transfers between devices: 197 us -> 0 us
  Pallas kernels: 0 us -> 33 us
  matrix products: 23.2 us -> 0 us
  between operations: 13.4 us -> 0.02 us
  local copies, waits for them, and re-layouts: 2.92 us -> 7.15 us
    reduce_scatter x1 -> x0, waiting for transfers between devices: 100 us -> none  [shards(): lax.psum_scatter(jnp.dot(col_feats.T, row_feats, precision=lax.Precision....]
    psum x1 -> x0, waiting for transfers between devices: 97.1 us -> none  [shards(): act_proj, grad_proj = lax.psum((act_part, grad_part), 'slab')]
    pallas_call x0 -> x2, Pallas kernels: none -> 33 us  [the longest x1 30.7 us: shards(): pl.pallas_call(functools.partial(exchange, blocks), out_shape=[jax.ShapeD...]
    dot_general x6 -> x0, matrix products: 23.2 us -> none  [the longest x1 15.9 us: shards(): jnp.dot(col_feats.T, row_feats, precision=lax.Precision.HIGHEST)]
    unnamed x5 -> x15, local copies, waits for them, and re-layouts: 0.78 us -> 7.15 us
  transfers between devices with their start and end apart: 2 -> 0, of which waited for: 2 -> 0; matrix products, arithmetic and copies ran while one was open for 0% -> 0% of each run, Pallas kernels for 0% -> 0%
where the time goes in v1:
time: 40.4 us; the launch traced here: 40.2 us
  Pallas kernels  33 us (82%)
  local copies, waits for them, and re-layouts  7.15 us (18%)
    pallas_call x1, Pallas kernels, shards(): pl.pallas_call(functools.partial(exchange, blocks), out_shape=[jax.ShapeD...  30.7 us
    unnamed x15, local copies, waits for them, and re-layouts  7.15 us
    pallas_call x1, Pallas kernels, shards(): pl.pallas_call(gram_block, out_shape=jax.ShapeDtypeStruct((wide, wide), F...  2.32 us

profile of v1, /device:TPU:1, one launch (start us, length us, event | category | flops | bytes accessed | tf_op | source)
XLA Modules:
  0.0 40.2 jit_solution(10733085242664985183)
XLA Ops:
  0.0 0.8 %copy.7.index = s32[14,2]{1,0:T(8,128)S(1)} copy(s32[14,2]{0,1:T(2,128)} %param.10) | data formatting | bytes 224 | tf_op args[4]
  0.8 0.0 copy-start
  0.8 1.5 %copy-done = bf16[512,1792]{1,0:T(8,128)(2,1)S(1)} copy-done((bf16[512,1792]{1,0:T(8,128)(2,1)S(1)}, bf16[512,1792]{1,0:T(8,128)(2,1)}, u32[]{:S(2)}) %copy-start) | copy-done | bytes 1835032
  2.3 0.0 copy-start.1
  2.3 1.0 %copy-done.1 = bf16[512,512]{1,0:T(8,128)(2,1)S(1)} copy-done((bf16[512,512]{1,0:T(8,128)(2,1)S(1)}, bf16[512,512]{1,0:T(8,128)(2,1)}, u32[]{:S(2)}) %copy-start.1) | copy-done | bytes 524312
  3.3 0.0 copy-start.4
  3.3 0.9 %copy-done.4 = bf16[128,512]{1,0:T(8,128)(2,1)S(1)} copy-done((bf16[128,512]{1,0:T(8,128)(2,1)S(1)}, bf16[128,512]{1,0:T(8,128)(2,1)}, u32[]{:S(2)}) %copy-start.4) | copy-done | bytes 131096
  4.2 0.0 copy-start.5
  4.2 0.9 %copy-done.5 = bf16[14,2,16,128]{3,2,1,0:T(8,128)(2,1)S(1)} copy-done((bf16[14,2,16,128]{3,2,1,0:T(8,128)(2,1)S(1)}, bf16[14,2,16,128]{3,2,1,0:T(8,128)(2,1)}, u32[]{:S(2)}) %copy-start.5) | copy-done | bytes 114712
  5.1 0.0 copy-start.6
  5.1 0.7 %copy-done.6 = s32[4]{0:T(128)S(1)} copy-done((s32[4]{0:T(128)S(1)}, s32[4]{0:T(128)}, u32[]{:S(2)}) %copy-start.6) | copy-done | bytes 40
  5.8 30.7 %exchange.1 = (bf16[256,512]{1,0:T(8,128)(2,1)S(1)}, bf16[256,512]{1,0:T(8,128)(2,1)S(1)}) custom-call(bf16[512,1792]{1,0:T(8,128)(2,1)S(1)} %copy-done, bf16[512,512]{1,0:T(8,128)(2,1)S(1)} %copy-done.1, bf16[128,512]{1,0:T(8,128)(2,1)S(1)} %copy-done.4, bf16[14,2,16,128]{3,2,1,0:T(8,128)(2,1)S(1)} %copy-done.5, s32[14,2]{1,0:T(8,128)S(1)} %copy.7.index, ...), custom_call_target="tpu_custom_call" | custom-call | tf_op jit(solution)/shard_map/exchange/pallas_call | solution.py:299
  36.5 0.0 copy-start.2
  36.5 0.7 %copy-done.2 = bf16[256,512]{1,0:T(8,128)(2,1)} copy-done((bf16[256,512]{1,0:T(8,128)(2,1)}, bf16[256,512]{1,0:T(8,128)(2,1)S(1)}, u32[]{:S(2)}) %copy-start.2) | copy-done | bytes 262168
  37.2 0.0 copy-start.3
  37.2 0.7 %copy-done.3 = bf16[256,512]{1,0:T(8,128)(2,1)} copy-done((bf16[256,512]{1,0:T(8,128)(2,1)}, bf16[256,512]{1,0:T(8,128)(2,1)S(1)}, u32[]{:S(2)}) %copy-start.3) | copy-done | bytes 262168
  37.9 2.3 %gram.1 = f32[512,512]{1,0:T(8,128)} custom-call(bf16[256,512]{1,0:T(8,128)(2,1)} %copy-done.2, bf16[256,512]{1,0:T(8,128)(2,1)} %copy-done.3), custom_call_target="tpu_custom_call" | custom-call | tf_op jit(solution)/shard_map/gram/pallas_call | solution.py:332
Async XLA Ops:
  0.8 1.5 %copy-start = (bf16[512,1792]{1,0:T(8,128)(2,1)S(1)}, bf16[512,1792]{1,0:T(8,128)(2,1)}, u32[]{:S(2)}) copy-start(bf16[512,1792]{1,0:T(8,128)(2,1)} %hidden.1) | copy-start | bytes 5505028
  2.3 1.0 %copy-start.1 = (bf16[512,512]{1,0:T(8,128)(2,1)S(1)}, bf16[512,512]{1,0:T(8,128)(2,1)}, u32[]{:S(2)}) copy-start(bf16[512,512]{1,0:T(8,128)(2,1)} %out_grad.1) | copy-start | bytes 1572868
  3.3 0.9 %copy-start.4 = (bf16[128,512]{1,0:T(8,128)(2,1)S(1)}, bf16[128,512]{1,0:T(8,128)(2,1)}, u32[]{:S(2)}) copy-start(bf16[128,512]{1,0:T(8,128)(2,1)} %right.1) | copy-start | bytes 393220
  4.2 0.9 %copy-start.5 = (bf16[14,2,16,128]{3,2,1,0:T(8,128)(2,1)S(1)}, bf16[14,2,16,128]{3,2,1,0:T(8,128)(2,1)}, u32[]{:S(2)}) copy-start(bf16[14,2,16,128]{3,2,1,0:T(8,128)(2,1)} %signs.1) | copy-start | bytes 344068
  5.1 0.7 %copy-start.6 = (s32[4]{0:T(128)S(1)}, s32[4]{0:T(128)}, u32[]{:S(2)}) copy-start(s32[4]{0:T(128)} %lengths.1) | copy-start | bytes 52
  36.5 0.7 %copy-start.2 = (bf16[256,512]{1,0:T(8,128)(2,1)}, bf16[256,512]{1,0:T(8,128)(2,1)S(1)}, u32[]{:S(2)}) copy-start(bf16[256,512]{1,0:T(8,128)(2,1)S(1)} %get-tuple-element.7.a_ref) | copy-start | bytes 786436
  37.2 0.7 %copy-start.3 = (bf16[256,512]{1,0:T(8,128)(2,1)}, bf16[256,512]{1,0:T(8,128)(2,1)S(1)}, u32[]{:S(2)}) copy-start(bf16[256,512]{1,0:T(8,128)(2,1)S(1)} %get-tuple-element.8.b_ref) | copy-start | bytes 786436

commit v2 on v0

v2 whole, which is shorter than its diff:
```python
import functools

import jax
import jax.numpy as jnp
from jax import lax
from jax.experimental import pallas as pl
from jax.experimental.pallas import tpu as pltpu
from jax.sharding import PartitionSpec as P

D = 8192
FF = 28672
SEQ = 128
BF = 128
KB = 4
BK = 16
K2 = 128
K1 = 64
EX_DEV = 4
PEERS = 16
ZS = 8
TOK = SEQ // 2
LANES = 128
HALF = LANES // 2
SCALE = FF**-0.5 * D**-0.5 * SEQ**-0.5

MESH = pl.DeviceIdType.MESH
F32 = jnp.float32
BF16 = jnp.bfloat16
NT = (((1,), (1,)), ((), ()))
TN = (((0,), (0,)), ((), ()))


def split(x):
    high = x.astype(BF16)
    return high, (x - high.astype(F32)).astype(BF16)


def remote(src, dst, send_sem, recv_sem, slab, ex):
    return pltpu.make_async_remote_copy(
        src_ref=src,
        dst_ref=dst,
        send_sem=send_sem,
        recv_sem=recv_sem,
        device_id=(slab, ex),
        device_id_type=MESH,
    )


def wait_bytes(ref, sem):
    pltpu.make_async_copy(ref, ref, sem).wait()


def place_halves(first, low, high):
    planes = [None] * EX_DEV
    for mm in range(2):
        planes[mm] = jnp.where(first, low[mm], pltpu.roll(high[mm], HALF, 1))
        planes[2 + mm] = jnp.where(first, pltpu.roll(low[mm], HALF, 1), high[mm])
    return jnp.concatenate(planes, axis=1)


def exchange(
    blocks,
    hidden,
    out_grad,
    right,
    signs,
    index,
    lengths,
    out,
    hid_v,
    og_v,
    right_v,
    signs_v,
    index_v,
    lengths_v,
    left_v,
    part,
    part_in,
    feat,
    row_in,
    c_buf,
    r_buf,
    hid_sem,
    og_sem,
    par_sem,
    send_sem,
    recv_sem,
):
    s = lax.axis_index("slab")
    e = lax.axis_index("ex")
    y, x = s // EX_DEV, s % EX_DEV
    low_half = s % 2 == 0

    barrier = pltpu.get_barrier_semaphore()

    @pl.loop(1, PEERS)
    def _(i):
        pl.semaphore_signal(
            barrier, inc=1, device_id=(lax.rem(s + i, PEERS), e), device_id_type=MESH
        )
        pl.semaphore_signal(
            barrier, inc=1, device_id=(s, lax.rem(e + i, PEERS)), device_id_type=MESH
        )

    par = [
        pltpu.make_async_copy(signs, signs_v, par_sem.at[0]),
        pltpu.make_async_copy(index, index_v, par_sem.at[1]),
        pltpu.make_async_copy(lengths, lengths_v, par_sem.at[2]),
        pltpu.make_async_copy(right, right_v, par_sem.at[3]),
    ]
    for copy in par:
        copy.start()
    owners = [lax.rem(y + 1 + i, EX_DEV) for i in range(EX_DEV)]
    copies = []
    for i, j in enumerate(owners):
        rows = pl.ds(pl.multiple_of(j * SEQ, SEQ), SEQ)
        pair = (
            pltpu.make_async_copy(hidden.at[rows], hid_v.at[i], hid_sem.at[i]),
            pltpu.make_async_copy(out_grad.at[rows], og_v.at[i], og_sem.at[i]),
        )
        for copy in pair:
            copy.start()
        copies.append(pair)

    par[0].wait()
    par[1].wait()
    for r in range(blocks):
        pair = [signs_v[r, n].astype(F32) for n in range(2)]
        for k in range(KB):
            on = [(index_v[n, r] == k).astype(F32) for n in range(2)]
            dense = (pair[0] * on[0] + pair[1] * on[1]).astype(BF16)
            cols = pl.ds(r * BF, BF)
            left_v[pl.ds(k * BK, BK), cols] = dense
            left_v[pl.ds(K1 + k * BK, BK), cols] = dense
    par[2].wait()
    par[3].wait()

    token = lax.broadcasted_iota(jnp.int32, (SEQ, LANES), 0)
    first = lax.broadcasted_iota(jnp.int32, (TOK, LANES), 1) < HALF
    for i, j in enumerate(owners):
        for copy in copies[i]:
            copy.wait()
        act = lax.dot_general(hid_v[i], left_v[...], NT, preferred_element_type=F32)
        act = jnp.where(token < lengths_v[j], act, 0.0)
        grad = lax.dot_general(og_v[i], right_v[...], NT, preferred_element_type=F32)
        for h in range(2):
            a, g = act[h * TOK : (h + 1) * TOK], grad[h * TOK : (h + 1) * TOK]
            part[i * EX_DEV + h * 2] = jnp.where(first, g, a)
            part[i * EX_DEV + h * 2 + 1] = jnp.where(first, a, g)
        if i == 0:
            pl.semaphore_wait(barrier, 2 * (PEERS - 1))
        for k in range(EX_DEV) if i < EX_DEV - 1 else range(1, EX_DEV):
            q = lax.rem(x + k, EX_DEV)
            remote(
                part.at[i * EX_DEV + q],
                part_in.at[s],
                send_sem.at[0],
                recv_sem.at[0],
                j * EX_DEV + q,
                e,
            ).start()
    part_in[s] = part[(EX_DEV - 1) * EX_DEV + x]
    wait_bytes(part_in.at[pl.ds(0, PEERS - 1)], recv_sem.at[0])

    total = part_in[0]
    for i in range(1, PEERS):
        total += part_in[i]
    high, low = split(total)
    outer = lax.dot_general(
        jnp.concatenate([high, high, low, low], axis=0),
        jnp.concatenate([high, low, high, low], axis=0),
        TN,
        preferred_element_type=F32,
    )
    mine = jnp.where(low_half, outer[K1:], outer[:K1]) * SCALE
    turned = pltpu.roll(mine, HALF, 1)
    lower = jnp.where(low_half, mine, turned)
    upper = jnp.where(low_half, turned, mine)
    packed = jnp.where(first, lower, pltpu.roll(upper, K1 - 2, 0))
    for i in range(PEERS):
        feat[i] = packed[i * EX_DEV : i * EX_DEV + 2]

    @pl.loop(1, PEERS)
    def _(i):
        to = lax.rem(e + i, PEERS)
        remote(feat.at[to], c_buf.at[s, e], send_sem.at[1], recv_sem.at[1], s, to).start()

    @pl.loop(1, PEERS)
    def _(i):
        to = lax.rem(s + i, PEERS)
        remote(feat.at[to], row_in.at[s], send_sem.at[2], recv_sem.at[2], to, e).start()

    c_buf[s, e] = feat[e]
    row_in[s] = feat[s]

    wait_bytes(row_in.at[pl.ds(0, PEERS - 1)], recv_sem.at[2])
    rows = [row_in[4 * j + b] + row_in[4 * j + 2 + b] for j in range(EX_DEV) for b in range(2)]
    own = pl.ds(pl.multiple_of(e * PEERS, PEERS), PEERS)
    r_buf[own] = jnp.concatenate(rows, axis=0)

    @pl.loop(1, PEERS)
    def _(i):
        to = lax.rem(e + i, PEERS)
        remote(r_buf.at[own], r_buf.at[own], send_sem.at[3], recv_sem.at[3], s, to).start()

    wait_bytes(c_buf.at[0, pl.ds(0, PEERS - 1)], recv_sem.at[1])

    @pl.loop(1, PEERS)
    def _(i):
        to = lax.rem(s + i, PEERS)
        remote(c_buf.at[s], c_buf.at[s], send_sem.at[4], recv_sem.at[4], to, e).start()

    wait_bytes(c_buf.at[pl.ds(0, PEERS - 1)], recv_sem.at[4])
    halves = []
    for b in range(2):
        sums = [c_buf[4 * j + b] + c_buf[4 * j + 2 + b] for j in range(EX_DEV)]
        halves.append([jnp.concatenate([t[:, mm] for t in sums], axis=0) for mm in range(2)])
    high, low = split(place_halves(first, *halves))
    col_side = jnp.concatenate([high, low, high, low], axis=0)

    wait_bytes(r_buf.at[pl.ds(0, (PEERS - 1) * PEERS)], recv_sem.at[3])
    halves = [
        [
            jnp.concatenate(
                [r_buf[pl.ds(4 * j + 2 * b + mm, PEERS, stride=PEERS), :] for j in range(EX_DEV)],
                axis=0,
            )
            for mm in range(2)
        ]
        for b in range(2)
    ]
    high, low = split(place_halves(first, *halves) * (1.0 / (PEERS * EX_DEV)))
    row_side = jnp.concatenate([high, high, low, low], axis=0)
    out[...] = lax.dot_general(row_side, col_side, TN, preferred_element_type=F32)

    wait_bytes(part.at[pl.ds(0, PEERS - 1)], send_sem.at[0])
    wait_bytes(feat.at[pl.ds(0, PEERS - 1)], send_sem.at[1])
    wait_bytes(feat.at[pl.ds(0, PEERS - 1)], send_sem.at[2])
    wait_bytes(r_buf.at[pl.ds(0, (PEERS - 1) * PEERS)], send_sem.at[3])
    wait_bytes(c_buf.at[pl.ds(0, PEERS - 1)], send_sem.at[4])


def shards(hidden, out_grad, lengths, left_signs, left_index, right_signs):
    tokens, ff = hidden.shape
    features = out_grad.shape[1]
    blocks = left_signs.shape[0]
    wide = EX_DEV * K2
    operands = (hidden, out_grad, right_signs, left_signs, left_index.T, lengths)
    return pl.pallas_call(
        functools.partial(exchange, blocks),
        out_shape=pltpu.VMEM((wide, wide), F32),
        in_specs=[pl.BlockSpec(memory_space=pltpu.HBM)] * 6,
        out_specs=pl.BlockSpec(memory_space=pltpu.VMEM),
        scratch_shapes=[
            pltpu.VMEM((EX_DEV, SEQ, ff), BF16),
            pltpu.VMEM((EX_DEV, SEQ, features), BF16),
            pltpu.VMEM((K2, features), BF16),
            pltpu.VMEM((blocks, 2, BK, BF), BF16),
            pltpu.SMEM((2, blocks), jnp.int32),
            pltpu.SMEM((EX_DEV,), jnp.int32),
            pltpu.VMEM((2 * K1, ff), BF16),
            pltpu.VMEM((PEERS, TOK, LANES), F32),
            pltpu.VMEM((PEERS, TOK, LANES), F32),
            pltpu.VMEM((PEERS, 2, LANES), F32),
            pltpu.VMEM((PEERS, 2, LANES), F32),
            pltpu.VMEM((PEERS, PEERS, 2, LANES), F32),
            pltpu.VMEM((PEERS * PEERS, LANES), F32),
            pltpu.SemaphoreType.DMA((EX_DEV,)),
            pltpu.SemaphoreType.DMA((EX_DEV,)),
            pltpu.SemaphoreType.DMA((4,)),
            pltpu.SemaphoreType.DMA((5,)),
            pltpu.SemaphoreType.DMA((5,)),
        ],
        compiler_params=pltpu.CompilerParams(
            collective_id=0, has_side_effects=True, vmem_limit_bytes=32 * 1024 * 1024
        ),
        name="exchange",
    )(*(pltpu.with_memory_space_constraint(a, pltpu.HBM) for a in operands))


def solution(mesh):
    in_specs = (
        P("ex", "slab"),
        P("ex", "slab"),
        P("ex"),
        P("slab", None, None, None),
        P("slab", None),
        P(None, "slab"),
    )
    out_specs = P("slab", "ex")
    return jax.shard_map(shards, mesh=mesh, in_specs=in_specs, out_specs=out_specs, check_vma=False)
```

time: 240 us -> 31.3 us (0.13)
  waiting for transfers between devices: 197 us -> 0 us
  Pallas kernels: 0 us -> 30.3 us
  matrix products: 23.2 us -> 0 us
  between operations: 13.4 us -> 0.01 us
    reduce_scatter x1 -> x0, waiting for transfers between devices: 100 us -> none  [shards(): lax.psum_scatter(jnp.dot(col_feats.T, row_feats, precision=lax.Precision....]
    psum x1 -> x0, waiting for transfers between devices: 97.1 us -> none  [shards(): act_proj, grad_proj = lax.psum((act_part, grad_part), 'slab')]
    pallas_call x0 -> x1, Pallas kernels: none -> 30.3 us  [shards(): pl.pallas_call(functools.partial(exchange, blocks), out_shape=pltpu.VMEM(...]
    dot_general x6 -> x0, matrix products: 23.2 us -> none  [the longest x1 15.9 us: shards(): jnp.dot(col_feats.T, row_feats, precision=lax.Precision.HIGHEST)]
  transfers between devices with their start and end apart: 2 -> 0, of which waited for: 2 -> 0; matrix products, arithmetic and copies ran while one was open for 0% -> 0% of each run, Pallas kernels for 0% -> 0%
where the time goes in v2:
time: 31.3 us; the launch traced here: 31.2 us
  Pallas kernels  30.3 us (97%)
  local copies, waits for them, and re-layouts  0.97 us (3%)
    pallas_call x1, Pallas kernels, shards(): pl.pallas_call(functools.partial(exchange, blocks), out_shape=pltpu.VMEM(...  30.3 us
    unnamed x1, local copies, waits for them, and re-layouts  0.97 us

profile of v2, /device:TPU:1, one launch (start us, length us, event | category | flops | bytes accessed | tf_op | source)
XLA Modules:
  0.0 31.2 jit_solution(6395263380323920923)
XLA Ops:
  0.0 30.3 %exchange.1 = f32[512,512]{1,0:T(8,128)S(1)} custom-call(bf16[512,1792]{1,0:T(8,128)(2,1)} %hidden.1, bf16[512,512]{1,0:T(8,128)(2,1)} %out_grad.1, bf16[128,512]{1,0:T(8,128)(2,1)} %right.1, bf16[14,2,16,128]{3,2,1,0:T(8,128)(2,1)} %signs.1, s32[2,14]{1,0:T(2,128)} %bitcast.1, s32[4]{0:T(128)} %lengths.1), custom_call_target="tpu_custom_call" | custom-call | tf_op jit(solution)/shard_map/exchange/pallas_call | solution.py:249
  30.3 1.0 %copy.8 = f32[512,512]{1,0:T(8,128)} copy(f32[512,512]{1,0:T(8,128)S(1)} %exchange.1) | data formatting | bytes 2097152

commit v3 on v2

v3 whole, which is shorter than its diff:
```python
import functools

import jax
import jax.numpy as jnp
from jax import lax
from jax.experimental import pallas as pl
from jax.experimental.pallas import tpu as pltpu
from jax.sharding import PartitionSpec as P

D = 8192
FF = 28672
SEQ = 128
BF = 128
KB = 4
BK = 16
K2 = 128
K1 = 64
EX_DEV = 4
PEERS = 16
ZS = 8
NEAR = (2, 6, 1, 7)
FAR = (4, 3, 5)
Y_ORDER = (2, 1, 3, 0)
X_ORDER = (2, 1, 3, 0)
COMPUTED = 0
TOK = SEQ // 4
CHUNK = TOK + TOK // 2
LANES = 128
HALF = LANES // 2
SCALE = FF**-0.5 * D**-0.5 * SEQ**-0.5

MESH = pl.DeviceIdType.MESH
F32 = jnp.float32
BF16 = jnp.bfloat16
NT = (((1,), (1,)), ((), ()))
TN = (((0,), (0,)), ((), ()))


def split(x):
    high = x.astype(BF16)
    return high, (x - high.astype(F32)).astype(BF16)


def remote(src, dst, send_sem, recv_sem, slab, ex):
    return pltpu.make_async_remote_copy(
        src_ref=src,
        dst_ref=dst,
        send_sem=send_sem,
        recv_sem=recv_sem,
        device_id=(slab, ex),
        device_id_type=MESH,
    )


def wait_bytes(ref, sem):
    pltpu.make_async_copy(ref, ref, sem).wait()


def group_slot(g):
    return lax.rem(g, EX_DEV) * EX_DEV + lax.div(g, EX_DEV)


def gather_rows(ref, stride, step):
    planes = []
    for m in range(EX_DEV):
        rows = [ref[pl.ds(j * step + m, PEERS, stride=stride), :] for j in range(EX_DEV)]
        planes.append(jnp.concatenate(rows, axis=0))
    return jnp.concatenate(planes, axis=1)


def exchange(
    blocks,
    hidden,
    out_grad,
    right,
    signs,
    index,
    lengths,
    out,
    hid_v,
    og_v,
    right_v,
    signs_v,
    index_v,
    lengths_v,
    left_v,
    part,
    part_in,
    feat,
    row_in,
    c_in,
    c_buf,
    r_buf,
    hid_sem,
    og_sem,
    par_sem,
    send_sem,
    recv_sem,
    ready,
):
    s = lax.axis_index("slab")
    e = lax.axis_index("ex")
    y, x = lax.div(s, EX_DEV), lax.rem(s, EX_DEV)
    z, c = lax.div(e, 2), lax.rem(e, 2)

    barrier = pltpu.get_barrier_semaphore()
    for i in range(1, PEERS):
        pl.semaphore_signal(
            barrier, inc=1, device_id=(lax.rem(s + i, PEERS), e), device_id_type=MESH
        )

    @pl.loop(e + 1, PEERS)
    def _(to):
        pl.semaphore_signal(barrier, inc=1, device_id=(s, to), device_id_type=MESH)

    par = [
        pltpu.make_async_copy(signs, signs_v, par_sem.at[0]),
        pltpu.make_async_copy(index, index_v, par_sem.at[1]),
        pltpu.make_async_copy(lengths, lengths_v, par_sem.at[2]),
        pltpu.make_async_copy(right, right_v, par_sem.at[3]),
    ]
    for copy in par:
        copy.start()
    owners = [lax.rem(y + i, EX_DEV) for i in Y_ORDER]
    copies = []
    for i, j in enumerate(owners):
        rows = pl.ds(pl.multiple_of(j * SEQ, SEQ), SEQ)
        pair = (
            pltpu.make_async_copy(hidden.at[rows], hid_v.at[i], hid_sem.at[i]),
            pltpu.make_async_copy(out_grad.at[rows], og_v.at[i], og_sem.at[i]),
        )
        for copy in pair:
            copy.start()
        copies.append(pair)

    par[0].wait()
    par[1].wait()
    for r in range(blocks):
        pair = [signs_v[r, n].astype(F32) for n in range(2)]
        for k in range(KB):
            on = [(index_v[n, r] == k).astype(F32) for n in range(2)]
            dense = (pair[0] * on[0] + pair[1] * on[1]).astype(BF16)
            cols = pl.ds(r * BF, BF)
            left_v[pl.ds(k * BK, BK), cols] = dense
            left_v[pl.ds(K1 + k * BK, BK), cols] = dense
    par[2].wait()
    par[3].wait()

    token = lax.broadcasted_iota(jnp.int32, (SEQ, LANES), 0)
    first = lax.broadcasted_iota(jnp.int32, (TOK // 2, LANES), 1) < HALF
    for i, j in enumerate(owners):
        for copy in copies[i]:
            copy.wait()
        act = lax.dot_general(hid_v[i], left_v[...], NT, preferred_element_type=F32)
        act = jnp.where(token < lengths_v[j], act, 0.0)
        grad = lax.dot_general(og_v[i], right_v[...], NT, preferred_element_type=F32)
        for q in range(EX_DEV):
            at = i * EX_DEV + q
            t = q * TOK
            part[at, :TOK] = grad[t : t + TOK]
            part[at, TOK:] = jnp.where(first, act[t : t + TOK // 2], act[t + TOK // 2 : t + TOK])
        if i == COMPUTED:
            pl.semaphore_wait(barrier, PEERS - 1 + e)

            @pl.loop(0, e)
            def _(to):
                pl.semaphore_signal(ready, inc=1, device_id=(s, to), device_id_type=MESH)

        if i < COMPUTED:
            continue
        for n in range(i + 1) if i == COMPUTED else (i,):
            for k in X_ORDER:
                if Y_ORDER[n] == 0 and k == 0:
                    continue
                q = lax.rem(x + k, EX_DEV)
                remote(
                    part.at[n * EX_DEV + q],
                    part_in.at[s],
                    send_sem.at[0],
                    recv_sem.at[0],
                    owners[n] * EX_DEV + q,
                    e,
                ).start()

    part_in[s] = part[Y_ORDER.index(0) * EX_DEV + x]
    wait_bytes(part_in.at[pl.ds(0, PEERS - 1)], recv_sem.at[0])

    total = part_in[0]
    for i in range(1, PEERS):
        total += part_in[i]
    packed = total[TOK:]
    acts = jnp.concatenate([jnp.where(first, packed, 0.0), jnp.where(first, 0.0, packed)], axis=0)
    act_h, act_l = split(acts)
    grad_h, grad_l = split(total[:TOK])
    outer = lax.dot_general(
        jnp.concatenate([act_h, act_h, act_l, act_l], axis=0),
        jnp.concatenate([grad_h, grad_l, grad_h, grad_l], axis=0),
        TN,
        preferred_element_type=F32,
    )
    features = (outer[:K1] + outer[K1:]) * SCALE
    for i in range(PEERS):
        feat[i] = features[i * EX_DEV : (i + 1) * EX_DEV]

    meet = y * EX_DEV + lax.rem(e, EX_DEV)
    spot = c_in.at[x, lax.div(e, EX_DEV)]

    def give(to):
        remote(feat.at[to], spot, send_sem.at[2], recv_sem.at[2], meet, to).start()

    pl.loop(0, e)(give)

    @pl.loop(1, PEERS)
    def _(i):
        to = lax.rem(s + i, PEERS)
        remote(feat.at[to], row_in.at[s], send_sem.at[1], recv_sem.at[1], to, e).start()


    @pl.when(e < PEERS - 1)
    def _():
        pl.semaphore_wait(ready, PEERS - 1 - e)

    pl.loop(e + 1, PEERS)(give)

    @pl.when(meet != s)
    def _():
        give(e)

    @pl.when(meet == s)
    def _():
        pltpu.make_async_copy(feat.at[e], spot, recv_sem.at[2]).start()

    row_in[s] = feat[s]
    wait_bytes(row_in.at[pl.ds(0, PEERS - 1)], recv_sem.at[1])
    rows = [
        row_in[4 * j] + row_in[4 * j + 1] + row_in[4 * j + 2] + row_in[4 * j + 3]
        for j in range(EX_DEV)
    ]
    def r_slot(g):
        return r_buf.at[pl.ds(pl.multiple_of(group_slot(g) * PEERS, PEERS), PEERS)]

    own = r_slot(e)
    own[...] = jnp.concatenate(rows, axis=0)

    def pass_on(g, sem, slab, ex):
        remote(r_slot(g), r_slot(g), send_sem.at[3], recv_sem.at[sem], slab, ex).start()

    for k in FAR:
        to = lax.rem(z + k, ZS) * 2
        pass_on(e, 3, s, to + c)
        pass_on(e, 3, s, to + 1 - c)
    for k in NEAR:
        pass_on(e, 4, s, lax.rem(z + k, ZS) * 2 + c)
    pass_on(e, 5, s, 2 * z + 1 - c)

    wait_bytes(c_in, recv_sem.at[2])
    c_buf[pl.ds(pl.multiple_of(s * PEERS, PEERS), PEERS)] = jnp.concatenate(
        [c_in[0, i] + c_in[1, i] + c_in[2, i] + c_in[3, i] for i in range(EX_DEV)], axis=0
    )
    at = c_buf.at[pl.ds(pl.multiple_of(s * PEERS, PEERS), PEERS)]

    @pl.loop(1, PEERS)
    def _(i):
        to = lax.rem(s + i, PEERS)
        remote(at, at, send_sem.at[4], recv_sem.at[6], to, e).start()

    wait_bytes(r_buf.at[pl.ds(0, len(NEAR) * PEERS)], recv_sem.at[4])
    for k in NEAR:
        pass_on(lax.rem(z + k, ZS) * 2 + c, 5, s, 2 * z + 1 - c)

    wait_bytes(c_buf.at[pl.ds(0, (PEERS - 1) * PEERS)], recv_sem.at[6])
    high, low = split(gather_rows(c_buf, EX_DEV, EX_DEV * PEERS))
    col_side = jnp.concatenate([high, low, high, low], axis=0)

    wait_bytes(r_buf.at[pl.ds(0, 2 * len(FAR) * PEERS)], recv_sem.at[3])
    wait_bytes(r_buf.at[pl.ds(0, (len(NEAR) + 1) * PEERS)], recv_sem.at[5])
    high, low = split(gather_rows(r_buf, PEERS, EX_DEV) * (1.0 / (PEERS * EX_DEV)))
    row_side = jnp.concatenate([high, high, low, low], axis=0)
    out[...] = lax.dot_general(row_side, col_side, TN, preferred_element_type=F32)

    wait_bytes(part.at[pl.ds(0, PEERS - 1)], send_sem.at[0])
    wait_bytes(feat.at[pl.ds(0, PEERS - 1)], send_sem.at[1])
    wait_bytes(feat.at[pl.ds(0, PEERS - 1)], send_sem.at[2])

    @pl.when(meet != s)
    def _():
        wait_bytes(feat.at[0], send_sem.at[2])

    wait_bytes(r_buf.at[pl.ds(0, (2 * len(FAR) + 2 * len(NEAR) + 1) * PEERS)], send_sem.at[3])
    wait_bytes(c_buf.at[pl.ds(0, (PEERS - 1) * PEERS)], send_sem.at[4])


def shards(hidden, out_grad, lengths, left_signs, left_index, right_signs):
    tokens, ff = hidden.shape
    features = out_grad.shape[1]
    blocks = left_signs.shape[0]
    wide = EX_DEV * K2
    operands = (hidden, out_grad, right_signs, left_signs, left_index.T, lengths)
    return pl.pallas_call(
        functools.partial(exchange, blocks),
        out_shape=pltpu.VMEM((wide, wide), F32),
        in_specs=[pl.BlockSpec(memory_space=pltpu.HBM)] * 6,
        out_specs=pl.BlockSpec(memory_space=pltpu.VMEM),
        scratch_shapes=[
            pltpu.VMEM((EX_DEV, SEQ, ff), BF16),
            pltpu.VMEM((EX_DEV, SEQ, features), BF16),
            pltpu.VMEM((K2, features), BF16),
            pltpu.VMEM((blocks, 2, BK, BF), BF16),
            pltpu.SMEM((2, blocks), jnp.int32),
            pltpu.SMEM((EX_DEV,), jnp.int32),
            pltpu.VMEM((2 * K1, ff), BF16),
            pltpu.VMEM((PEERS, CHUNK, LANES), F32),
            pltpu.VMEM((PEERS, CHUNK, LANES), F32),
            pltpu.VMEM((PEERS, EX_DEV, K2), F32),
            pltpu.VMEM((PEERS, EX_DEV, K2), F32),
            pltpu.VMEM((EX_DEV, EX_DEV, EX_DEV, K2), F32),
            pltpu.VMEM((PEERS * PEERS, K2), F32),
            pltpu.VMEM((PEERS * PEERS, K2), F32),
            pltpu.SemaphoreType.DMA((EX_DEV,)),
            pltpu.SemaphoreType.DMA((EX_DEV,)),
            pltpu.SemaphoreType.DMA((4,)),
            pltpu.SemaphoreType.DMA((5,)),
            pltpu.SemaphoreType.DMA((7,)),
            pltpu.SemaphoreType.REGULAR,
        ],
        compiler_params=pltpu.CompilerParams(
            collective_id=0, has_side_effects=True, vmem_limit_bytes=32 * 1024 * 1024
        ),
        name="exchange",
    )(*(pltpu.with_memory_space_constraint(a, pltpu.HBM) for a in operands))


def solution(mesh):
    in_specs = (
        P("ex", "slab"),
        P("ex", "slab"),
        P("ex"),
        P("slab", None, None, None),
        P("slab", None),
        P(None, "slab"),
    )
    out_specs = P("slab", "ex")
    return jax.shard_map(shards, mesh=mesh, in_specs=in_specs, out_specs=out_specs, check_vma=False)
```

time: 31.3 us -> 29.1 us (0.930)
  Pallas kernels: 30.3 us -> 28.1 us
    pallas_call x1, Pallas kernels: 30.3 us -> 28.1 us  [shards(): pl.pallas_call(functools.partial(exchange, blocks), out_shape=pltpu.VMEM(...]
where the time goes in v3:
time: 29.1 us; the launch traced here: 29 us
  Pallas kernels  28.1 us (97%)
  local copies, waits for them, and re-layouts  0.97 us (3%)
    pallas_call x1, Pallas kernels, shards(): pl.pallas_call(functools.partial(exchange, blocks), out_shape=pltpu.VMEM(...  28.1 us
    unnamed x1, local copies, waits for them, and re-layouts  0.97 us

profile of v3, /device:TPU:1, one launch (start us, length us, event | category | flops | bytes accessed | tf_op | source)
XLA Modules:
  0.0 29.0 jit_solution(14294581342746058055)
XLA Ops:
  0.0 28.1 %exchange.1 = f32[512,512]{1,0:T(8,128)S(1)} custom-call(bf16[512,1792]{1,0:T(8,128)(2,1)} %hidden.1, bf16[512,512]{1,0:T(8,128)(2,1)} %out_grad.1, bf16[128,512]{1,0:T(8,128)(2,1)} %right.1, bf16[14,2,16,128]{3,2,1,0:T(8,128)(2,1)} %signs.1, s32[2,14]{1,0:T(2,128)} %bitcast.1, s32[4]{0:T(128)} %lengths.1), custom_call_target="tpu_custom_call" | custom-call | tf_op jit(solution)/shard_map/exchange/pallas_call | solution.py:299
  28.1 1.0 %copy.8 = f32[512,512]{1,0:T(8,128)} copy(f32[512,512]{1,0:T(8,128)S(1)} %exchange.1) | data formatting | bytes 2097152

commit v4 on v3

--- a/solution.py
+++ b/solution.py
@@ -18,8 +18,7 @@
 EX_DEV = 4
 PEERS = 16
 ZS = 8
-NEAR = (2, 6, 1, 7)
-FAR = (4, 3, 5)
+Z_ORDER = (4, 3, 5, 2, 6, 1, 7)
 Y_ORDER = (2, 1, 3, 0)
 X_ORDER = (2, 1, 3, 0)
 COMPUTED = 0
@@ -54,10 +53,6 @@
 
 def wait_bytes(ref, sem):
     pltpu.make_async_copy(ref, ref, sem).wait()
-
-
-def group_slot(g):
-    return lax.rem(g, EX_DEV) * EX_DEV + lax.div(g, EX_DEV)
 
 
 def gather_rows(ref, stride, step):
@@ -236,22 +231,18 @@
         row_in[4 * j] + row_in[4 * j + 1] + row_in[4 * j + 2] + row_in[4 * j + 3]
         for j in range(EX_DEV)
     ]
-    def r_slot(g):
-        return r_buf.at[pl.ds(pl.multiple_of(group_slot(g) * PEERS, PEERS), PEERS)]
-
-    own = r_slot(e)
+    slot = lax.rem(e, EX_DEV) * EX_DEV + lax.div(e, EX_DEV)
+    own = r_buf.at[pl.ds(pl.multiple_of(slot * PEERS, PEERS), PEERS)]
     own[...] = jnp.concatenate(rows, axis=0)
 
-    def pass_on(g, sem, slab, ex):
-        remote(r_slot(g), r_slot(g), send_sem.at[3], recv_sem.at[sem], slab, ex).start()
-
-    for k in FAR:
+    def pass_on(ex):
+        remote(own, own, send_sem.at[3], recv_sem.at[3], s, ex).start()
+
+    for k in Z_ORDER:
         to = lax.rem(z + k, ZS) * 2
-        pass_on(e, 3, s, to + c)
-        pass_on(e, 3, s, to + 1 - c)
-    for k in NEAR:
-        pass_on(e, 4, s, lax.rem(z + k, ZS) * 2 + c)
-    pass_on(e, 5, s, 2 * z + 1 - c)
+        pass_on(to + c)
+        pass_on(to + 1 - c)
+    pass_on(2 * z + 1 - c)
 
     wait_bytes(c_in, recv_sem.at[2])
     c_buf[pl.ds(pl.multiple_of(s * PEERS, PEERS), PEERS)] = jnp.concatenate(
@@ -262,20 +253,16 @@
     @pl.loop(1, PEERS)
     def _(i):
         to = lax.rem(s + i, PEERS)
-        remote(at, at, send_sem.at[4], recv_sem.at[6], to, e).start()
-
-    wait_bytes(r_buf.at[pl.ds(0, len(NEAR) * PEERS)], recv_sem.at[4])
-    for k in NEAR:
-        pass_on(lax.rem(z + k, ZS) * 2 + c, 5, s, 2 * z + 1 - c)
-
-    wait_bytes(c_buf.at[pl.ds(0, (PEERS - 1) * PEERS)], recv_sem.at[6])
+        remote(at, at, send_sem.at[4], recv_sem.at[4], to, e).start()
+
+
+    wait_bytes(r_buf.at[pl.ds(0, (PEERS - 1) * PEERS)], recv_sem.at[3])
+    high, low = split(gather_rows(r_buf, PEERS, EX_DEV) * (1.0 / (PEERS * EX_DEV)))
+    row_side = jnp.concatenate([high, high, low, low], axis=0)
+    wait_bytes(c_buf.at[pl.ds(0, (PEERS - 1) * PEERS)], recv_sem.at[4])
     high, low = split(gather_rows(c_buf, EX_DEV, EX_DEV * PEERS))
     col_side = jnp.concatenate([high, low, high, low], axis=0)
 
-    wait_bytes(r_buf.at[pl.ds(0, 2 * len(FAR) * PEERS)], recv_sem.at[3])
-    wait_bytes(r_buf.at[pl.ds(0, (len(NEAR) + 1) * PEERS)], recv_sem.at[5])
-    high, low = split(gather_rows(r_buf, PEERS, EX_DEV) * (1.0 / (PEERS * EX_DEV)))
-    row_side = jnp.concatenate([high, high, low, low], axis=0)
     out[...] = lax.dot_general(row_side, col_side, TN, preferred_element_type=F32)
 
     wait_bytes(part.at[pl.ds(0, PEERS - 1)], send_sem.at[0])
@@ -286,7 +273,7 @@
     def _():
         wait_bytes(feat.at[0], send_sem.at[2])
 
-    wait_bytes(r_buf.at[pl.ds(0, (2 * len(FAR) + 2 * len(NEAR) + 1) * PEERS)], send_sem.at[3])
+    wait_bytes(r_buf.at[pl.ds(0, (PEERS - 1) * PEERS)], send_sem.at[3])
     wait_bytes(c_buf.at[pl.ds(0, (PEERS - 1) * PEERS)], send_sem.at[4])
 
 
@@ -320,7 +307,7 @@
             pltpu.SemaphoreType.DMA((EX_DEV,)),
             pltpu.SemaphoreType.DMA((4,)),
             pltpu.SemaphoreType.DMA((5,)),
-            pltpu.SemaphoreType.DMA((7,)),
+            pltpu.SemaphoreType.DMA((5,)),
             pltpu.SemaphoreType.REGULAR,
         ],
         compiler_params=pltpu.CompilerParams(

time: 29.1 us -> 28.6 us (0.983)
  Pallas kernels: 28.1 us -> 27.5 us
    pallas_call x1, Pallas kernels: 28.1 us -> 27.5 us  [shards(): pl.pallas_call(functools.partial(exchange, blocks), out_shape=pltpu.VMEM(...]
where the time goes in v4:
time: 28.6 us; the launch traced here: 28.5 us
  Pallas kernels  27.5 us (96%)
  local copies, waits for them, and re-layouts  0.97 us (3%)
    pallas_call x1, Pallas kernels, shards(): pl.pallas_call(functools.partial(exchange, blocks), out_shape=pltpu.VMEM(...  27.5 us
    unnamed x1, local copies, waits for them, and re-layouts  0.97 us

profile of v4, /device:TPU:1, one launch (start us, length us, event | category | flops | bytes accessed | tf_op | source)
XLA Modules:
  0.0 28.5 jit_solution(10940530398287528581)
XLA Ops:
  0.0 27.5 %exchange.1 = f32[512,512]{1,0:T(8,128)S(1)} custom-call(bf16[512,1792]{1,0:T(8,128)(2,1)} %hidden.1, bf16[512,512]{1,0:T(8,128)(2,1)} %out_grad.1, bf16[128,512]{1,0:T(8,128)(2,1)} %right.1, bf16[14,2,16,128]{3,2,1,0:T(8,128)(2,1)} %signs.1, s32[2,14]{1,0:T(2,128)} %bitcast.1, s32[4]{0:T(128)} %lengths.1), custom_call_target="tpu_custom_call" | custom-call | tf_op jit(solution)/shard_map/exchange/pallas_call | solution.py:286
  27.5 1.0 %copy.8 = f32[512,512]{1,0:T(8,128)} copy(f32[512,512]{1,0:T(8,128)S(1)} %exchange.1) | data formatting | bytes 2097152

commit v5 on v4

--- a/solution.py
+++ b/solution.py
@@ -19,7 +19,8 @@
 PEERS = 16
 ZS = 8
 Z_ORDER = (4, 3, 5, 2, 6, 1, 7)
-Y_ORDER = (2, 1, 3, 0)
+Y_ORDER = (2, 3, 1, 0)
+LEAD = (0, 1)
 X_ORDER = (2, 1, 3, 0)
 COMPUTED = 0
 TOK = SEQ // 4
@@ -61,6 +62,16 @@
         rows = [ref[pl.ds(j * step + m, PEERS, stride=stride), :] for j in range(EX_DEV)]
         planes.append(jnp.concatenate(rows, axis=0))
     return jnp.concatenate(planes, axis=1)
+
+
+def add_quarters(ref):
+    planes = [[] for _ in range(EX_DEV)]
+    for j in range(EX_DEV):
+        at = [ref[pl.ds((EX_DEV * j + q) * PEERS, PEERS)] for q in range(EX_DEV)]
+        total = at[0] + at[1] + at[2] + at[3]
+        for m in range(EX_DEV):
+            planes[m].append(total[:, m])
+    return jnp.concatenate([jnp.concatenate(rows, axis=0) for rows in planes], axis=1)
 
 
 def exchange(
@@ -86,6 +97,7 @@
     c_in,
     c_buf,
     r_buf,
+    lead_in,
     hid_sem,
     og_sem,
     par_sem,
@@ -97,6 +109,11 @@
     e = lax.axis_index("ex")
     y, x = lax.div(s, EX_DEV), lax.rem(s, EX_DEV)
     z, c = lax.div(e, 2), lax.rem(e, 2)
+
+    def is_lead(slab, ex):
+        return jnp.logical_and(slab == LEAD[0], ex == LEAD[1])
+
+    lead = is_lead(s, e)
 
     barrier = pltpu.get_barrier_semaphore()
     for i in range(1, PEERS):
@@ -197,6 +214,18 @@
     for i in range(PEERS):
         feat[i] = features[i * EX_DEV : (i + 1) * EX_DEV]
 
+    def to_lead():
+        for k in range(2):
+            remote(
+                feat.at[LEAD[k]],
+                lead_in.at[k, s * PEERS + e],
+                send_sem.at[5],
+                recv_sem.at[5 + k],
+                *LEAD,
+            ).start()
+
+    pl.when(e > LEAD[1])(to_lead)
+
     meet = y * EX_DEV + lax.rem(e, EX_DEV)
     spot = c_in.at[x, lax.div(e, EX_DEV)]
 
@@ -214,6 +243,15 @@
     @pl.when(e < PEERS - 1)
     def _():
         pl.semaphore_wait(ready, PEERS - 1 - e)
+
+    @pl.when(jnp.logical_and(e <= LEAD[1], jnp.logical_not(lead)))
+    def _():
+        to_lead()
+
+    @pl.when(lead)
+    def _():
+        for k in range(2):
+            lead_in[k, LEAD[0] * PEERS + LEAD[1]] = feat[LEAD[k]]
 
     pl.loop(e + 1, PEERS)(give)
 
@@ -236,7 +274,9 @@
     own[...] = jnp.concatenate(rows, axis=0)
 
     def pass_on(ex):
-        remote(own, own, send_sem.at[3], recv_sem.at[3], s, ex).start()
+        @pl.when(jnp.logical_not(is_lead(s, ex)))
+        def _():
+            remote(own, own, send_sem.at[3], recv_sem.at[3], s, ex).start()
 
     for k in Z_ORDER:
         to = lax.rem(z + k, ZS) * 2
@@ -253,17 +293,36 @@
     @pl.loop(1, PEERS)
     def _(i):
         to = lax.rem(s + i, PEERS)
-        remote(at, at, send_sem.at[4], recv_sem.at[4], to, e).start()
-
-
-    wait_bytes(r_buf.at[pl.ds(0, (PEERS - 1) * PEERS)], recv_sem.at[3])
-    high, low = split(gather_rows(r_buf, PEERS, EX_DEV) * (1.0 / (PEERS * EX_DEV)))
-    row_side = jnp.concatenate([high, high, low, low], axis=0)
-    wait_bytes(c_buf.at[pl.ds(0, (PEERS - 1) * PEERS)], recv_sem.at[4])
-    high, low = split(gather_rows(c_buf, EX_DEV, EX_DEV * PEERS))
-    col_side = jnp.concatenate([high, low, high, low], axis=0)
-
-    out[...] = lax.dot_general(row_side, col_side, TN, preferred_element_type=F32)
+
+        @pl.when(jnp.logical_not(is_lead(to, e)))
+        def _():
+            remote(at, at, send_sem.at[4], recv_sem.at[4], to, e).start()
+
+
+    def gram(row_side, wait, cols):
+        high, low = split(row_side * (1.0 / (PEERS * EX_DEV)))
+        row_side = jnp.concatenate([high, high, low, low], axis=0)
+        wait()
+        high, low = split(cols())
+        col_side = jnp.concatenate([high, low, high, low], axis=0)
+        out[...] = lax.dot_general(row_side, col_side, TN, preferred_element_type=F32)
+
+    @pl.when(jnp.logical_not(lead))
+    def _():
+        wait_bytes(r_buf.at[pl.ds(0, (PEERS - 1) * PEERS)], recv_sem.at[3])
+        gram(
+            gather_rows(r_buf, PEERS, EX_DEV),
+            lambda: wait_bytes(c_buf.at[pl.ds(0, (PEERS - 1) * PEERS)], recv_sem.at[4]),
+            lambda: gather_rows(c_buf, EX_DEV, EX_DEV * PEERS),
+        )
+
+    @pl.when(lead)
+    def _():
+        def arrive(k):
+            wait_bytes(lead_in.at[k, pl.ds(0, PEERS * PEERS - 1)], recv_sem.at[5 + k])
+
+        arrive(0)
+        gram(add_quarters(lead_in.at[0]), lambda: arrive(1), lambda: add_quarters(lead_in.at[1]))
 
     wait_bytes(part.at[pl.ds(0, PEERS - 1)], send_sem.at[0])
     wait_bytes(feat.at[pl.ds(0, PEERS - 1)], send_sem.at[1])
@@ -273,8 +332,20 @@
     def _():
         wait_bytes(feat.at[0], send_sem.at[2])
 
-    wait_bytes(r_buf.at[pl.ds(0, (PEERS - 1) * PEERS)], send_sem.at[3])
-    wait_bytes(c_buf.at[pl.ds(0, (PEERS - 1) * PEERS)], send_sem.at[4])
+    wait_bytes(r_buf.at[pl.ds(0, (PEERS - 2) * PEERS)], send_sem.at[3])
+    wait_bytes(c_buf.at[pl.ds(0, (PEERS - 2) * PEERS)], send_sem.at[4])
+
+    @pl.when(jnp.logical_or(s != LEAD[0], lead))
+    def _():
+        wait_bytes(r_buf.at[pl.ds(0, PEERS)], send_sem.at[3])
+
+    @pl.when(jnp.logical_or(e != LEAD[1], lead))
+    def _():
+        wait_bytes(c_buf.at[pl.ds(0, PEERS)], send_sem.at[4])
+
+    @pl.when(jnp.logical_not(lead))
+    def _():
+        wait_bytes(lead_in.at[0, pl.ds(0, 2)], send_sem.at[5])
 
 
 def shards(hidden, out_grad, lengths, left_signs, left_index, right_signs):
@@ -303,11 +374,12 @@
             pltpu.VMEM((EX_DEV, EX_DEV, EX_DEV, K2), F32),
             pltpu.VMEM((PEERS * PEERS, K2), F32),
             pltpu.VMEM((PEERS * PEERS, K2), F32),
+            pltpu.VMEM((2, PEERS * PEERS, EX_DEV, K2), F32),
             pltpu.SemaphoreType.DMA((EX_DEV,)),
             pltpu.SemaphoreType.DMA((EX_DEV,)),
             pltpu.SemaphoreType.DMA((4,)),
-            pltpu.SemaphoreType.DMA((5,)),
-            pltpu.SemaphoreType.DMA((5,)),
+            pltpu.SemaphoreType.DMA((6,)),
+            pltpu.SemaphoreType.DMA((7,)),
             pltpu.SemaphoreType.REGULAR,
         ],
         compiler_params=pltpu.CompilerParams(

time: 28.6 us -> 27.9 us (0.976)
  the two profiles are of different devices: /device:TPU:1 before, /device:TPU:32 now
where the time goes in v5:
time: 27.9 us; the launch traced here: 27.8 us
  Pallas kernels  26.9 us (96%)
  local copies, waits for them, and re-layouts  0.97 us (3%)
    pallas_call x1, Pallas kernels, shards(): pl.pallas_call(functools.partial(exchange, blocks), out_shape=pltpu.VMEM(...  26.9 us
    unnamed x1, local copies, waits for them, and re-layouts  0.97 us

profile of v5, /device:TPU:32, one launch (start us, length us, event | category | flops | bytes accessed | tf_op | source)
XLA Modules:
  0.0 27.8 jit_solution(14244915062048680109)
XLA Ops:
  0.0 26.9 %exchange.1 = f32[512,512]{1,0:T(8,128)S(1)} custom-call(bf16[512,1792]{1,0:T(8,128)(2,1)} %hidden.1, bf16[512,512]{1,0:T(8,128)(2,1)} %out_grad.1, bf16[128,512]{1,0:T(8,128)(2,1)} %right.1, bf16[14,2,16,128]{3,2,1,0:T(8,128)(2,1)} %signs.1, s32[2,14]{1,0:T(2,128)} %bitcast.1, s32[4]{0:T(128)} %lengths.1), custom_call_target="tpu_custom_call" | custom-call | tf_op jit(solution)/shard_map/exchange/pallas_call | solution.py:357
  26.9 1.0 %copy.8 = f32[512,512]{1,0:T(8,128)} copy(f32[512,512]{1,0:T(8,128)S(1)} %exchange.1) | data formatting | bytes 2097152

commit v6 on v5

--- a/solution.py
+++ b/solution.py
@@ -20,7 +20,7 @@
 ZS = 8
 Z_ORDER = (4, 3, 5, 2, 6, 1, 7)
 Y_ORDER = (2, 3, 1, 0)
-LEAD = (0, 1)
+LEADS = ((1, 3), (0, 1), (0, 1), (0, 0), (0, 1))
 X_ORDER = (2, 1, 3, 0)
 COMPUTED = 0
 TOK = SEQ // 4
@@ -62,6 +62,18 @@
         rows = [ref[pl.ds(j * step + m, PEERS, stride=stride), :] for j in range(EX_DEV)]
         planes.append(jnp.concatenate(rows, axis=0))
     return jnp.concatenate(planes, axis=1)
+
+
+def leads_of(slab):
+    low = high = jnp.int32(0)
+    for k, (first, last) in enumerate(LEADS):
+        low = jnp.where(slab == k, first, low)
+        high = jnp.where(slab == k, last, high)
+    return low, high
+
+
+def within(ex, limits):
+    return jnp.logical_and(ex >= limits[0], ex < limits[1])
 
 
 def add_quarters(ref):
@@ -110,10 +122,8 @@
     y, x = lax.div(s, EX_DEV), lax.rem(s, EX_DEV)
     z, c = lax.div(e, 2), lax.rem(e, 2)
 
-    def is_lead(slab, ex):
-        return jnp.logical_and(slab == LEAD[0], ex == LEAD[1])
-
-    lead = is_lead(s, e)
+    row_leads = leads_of(s)
+    lead = within(e, row_leads)
 
     barrier = pltpu.get_barrier_semaphore()
     for i in range(1, PEERS):
@@ -214,17 +224,27 @@
     for i in range(PEERS):
         feat[i] = features[i * EX_DEV : (i + 1) * EX_DEV]
 
-    def to_lead():
-        for k in range(2):
-            remote(
-                feat.at[LEAD[k]],
-                lead_in.at[k, s * PEERS + e],
-                send_sem.at[5],
-                recv_sem.at[5 + k],
-                *LEAD,
-            ).start()
-
-    pl.when(e > LEAD[1])(to_lead)
+    def to_leads(slabs):
+        for k in slabs:
+            limits = LEADS[k]
+
+            @pl.loop(*limits)
+            def _(to):
+                @pl.when(jnp.logical_or(s != k, e != to))
+                def _():
+                    for side, at in enumerate((k, to)):
+                        remote(
+                            feat.at[at],
+                            lead_in.at[side, s * PEERS + e],
+                            send_sem.at[5],
+                            recv_sem.at[5 + side],
+                            k,
+                            to,
+                        ).start()
+
+    @pl.when(e >= PEERS // 2)
+    def _():
+        to_leads((0,))
 
     meet = y * EX_DEV + lax.rem(e, EX_DEV)
     spot = c_in.at[x, lax.div(e, EX_DEV)]
@@ -244,24 +264,26 @@
     def _():
         pl.semaphore_wait(ready, PEERS - 1 - e)
 
-    @pl.when(jnp.logical_and(e <= LEAD[1], jnp.logical_not(lead)))
-    def _():
-        to_lead()
+    pl.loop(e + 1, PEERS)(give)
+
+    @pl.when(meet != s)
+    def _():
+        give(e)
+
+    @pl.when(meet == s)
+    def _():
+        pltpu.make_async_copy(feat.at[e], spot, recv_sem.at[2]).start()
+
+    @pl.when(e < PEERS // 2)
+    def _():
+        to_leads((0,))
+
+    to_leads(range(1, len(LEADS)))
 
     @pl.when(lead)
     def _():
-        for k in range(2):
-            lead_in[k, LEAD[0] * PEERS + LEAD[1]] = feat[LEAD[k]]
-
-    pl.loop(e + 1, PEERS)(give)
-
-    @pl.when(meet != s)
-    def _():
-        give(e)
-
-    @pl.when(meet == s)
-    def _():
-        pltpu.make_async_copy(feat.at[e], spot, recv_sem.at[2]).start()
+        lead_in[0, s * PEERS + e] = feat[s]
+        lead_in[1, s * PEERS + e] = feat[e]
 
     row_in[s] = feat[s]
     wait_bytes(row_in.at[pl.ds(0, PEERS - 1)], recv_sem.at[1])
@@ -274,7 +296,7 @@
     own[...] = jnp.concatenate(rows, axis=0)
 
     def pass_on(ex):
-        @pl.when(jnp.logical_not(is_lead(s, ex)))
+        @pl.when(jnp.logical_not(within(ex, row_leads)))
         def _():
             remote(own, own, send_sem.at[3], recv_sem.at[3], s, ex).start()
 
@@ -294,7 +316,7 @@
     def _(i):
         to = lax.rem(s + i, PEERS)
 
-        @pl.when(jnp.logical_not(is_lead(to, e)))
+        @pl.when(jnp.logical_not(within(e, leads_of(to))))
         def _():
             remote(at, at, send_sem.at[4], recv_sem.at[4], to, e).start()
 
@@ -332,16 +354,21 @@
     def _():
         wait_bytes(feat.at[0], send_sem.at[2])
 
-    wait_bytes(r_buf.at[pl.ds(0, (PEERS - 2) * PEERS)], send_sem.at[3])
-    wait_bytes(c_buf.at[pl.ds(0, (PEERS - 2) * PEERS)], send_sem.at[4])
-
-    @pl.when(jnp.logical_or(s != LEAD[0], lead))
-    def _():
-        wait_bytes(r_buf.at[pl.ds(0, PEERS)], send_sem.at[3])
-
-    @pl.when(jnp.logical_or(e != LEAD[1], lead))
-    def _():
-        wait_bytes(c_buf.at[pl.ds(0, PEERS)], send_sem.at[4])
+    others = PEERS - (row_leads[1] - row_leads[0]) - jnp.where(lead, 0, 1)
+
+    @pl.loop(0, others)
+    def _(k):
+        wait_bytes(own, send_sem.at[3])
+
+    reached = PEERS - jnp.where(lead, 0, 1)
+    for limits in LEADS:
+        reached -= within(e, limits).astype(jnp.int32)
+
+    @pl.loop(0, reached)
+    def _(k):
+        wait_bytes(at, send_sem.at[4])
+
+    wait_bytes(lead_in.at[0, pl.ds(0, 2 * (sum(high - low for low, high in LEADS) - 1))], send_sem.at[5])
 
     @pl.when(jnp.logical_not(lead))
     def _():

time: 27.9 us -> 27.6 us (0.989)
  the two profiles are of different devices: /device:TPU:32 before, /device:TPU:64 now
where the time goes in v6:
time: 27.6 us; the launch traced here: 27.5 us
  Pallas kernels  26.5 us (96%)
  local copies, waits for them, and re-layouts  0.97 us (4%)
    pallas_call x1, Pallas kernels, shards(): pl.pallas_call(functools.partial(exchange, blocks), out_shape=pltpu.VMEM(...  26.5 us
    unnamed x1, local copies, waits for them, and re-layouts  0.97 us

profile of v6, /device:TPU:64, one launch (start us, length us, event | category | flops | bytes accessed | tf_op | source)
XLA Modules:
  0.0 27.5 jit_solution(9231547647978806182)
XLA Ops:
  0.0 26.5 %exchange.1 = f32[512,512]{1,0:T(8,128)S(1)} custom-call(bf16[512,1792]{1,0:T(8,128)(2,1)} %hidden.1, bf16[512,512]{1,0:T(8,128)(2,1)} %out_grad.1, bf16[128,512]{1,0:T(8,128)(2,1)} %right.1, bf16[14,2,16,128]{3,2,1,0:T(8,128)(2,1)} %signs.1, s32[2,14]{1,0:T(2,128)} %bitcast.1, s32[4]{0:T(128)} %lengths.1), custom_call_target="tpu_custom_call" | custom-call | tf_op jit(solution)/shard_map/exchange/pallas_call | solution.py:384
  26.5 1.0 %copy.8 = f32[512,512]{1,0:T(8,128)} copy(f32[512,512]{1,0:T(8,128)S(1)} %exchange.1) | data formatting | bytes 2097152

commit v7 on v6

--- a/solution.py
+++ b/solution.py
@@ -22,7 +22,7 @@
 Y_ORDER = (2, 3, 1, 0)
 LEADS = ((1, 3), (0, 1), (0, 1), (0, 0), (0, 1))
 X_ORDER = (2, 1, 3, 0)
-COMPUTED = 0
+COMPUTED = 1
 TOK = SEQ // 4
 CHUNK = TOK + TOK // 2
 LANES = 128
@@ -321,6 +321,34 @@
             remote(at, at, send_sem.at[4], recv_sem.at[4], to, e).start()
 
 
+    wait_bytes(part.at[pl.ds(0, PEERS - 1)], send_sem.at[0])
+    wait_bytes(feat.at[pl.ds(0, PEERS - 1)], send_sem.at[1])
+    wait_bytes(feat.at[pl.ds(0, PEERS - 1)], send_sem.at[2])
+
+    @pl.when(meet != s)
+    def _():
+        wait_bytes(feat.at[0], send_sem.at[2])
+
+    others = PEERS - (row_leads[1] - row_leads[0]) - jnp.where(lead, 0, 1)
+
+    @pl.loop(0, others)
+    def _(k):
+        wait_bytes(own, send_sem.at[3])
+
+    reached = PEERS - jnp.where(lead, 0, 1)
+    for limits in LEADS:
+        reached -= within(e, limits).astype(jnp.int32)
+
+    @pl.loop(0, reached)
+    def _(k):
+        wait_bytes(at, send_sem.at[4])
+
+    wait_bytes(lead_in.at[0, pl.ds(0, 2 * (sum(high - low for low, high in LEADS) - 1))], send_sem.at[5])
+
+    @pl.when(jnp.logical_not(lead))
+    def _():
+        wait_bytes(lead_in.at[0, pl.ds(0, 2)], send_sem.at[5])
+
     def gram(row_side, wait, cols):
         high, low = split(row_side * (1.0 / (PEERS * EX_DEV)))
         row_side = jnp.concatenate([high, high, low, low], axis=0)
@@ -345,34 +373,6 @@
 
         arrive(0)
         gram(add_quarters(lead_in.at[0]), lambda: arrive(1), lambda: add_quarters(lead_in.at[1]))
-
-    wait_bytes(part.at[pl.ds(0, PEERS - 1)], send_sem.at[0])
-    wait_bytes(feat.at[pl.ds(0, PEERS - 1)], send_sem.at[1])
-    wait_bytes(feat.at[pl.ds(0, PEERS - 1)], send_sem.at[2])
-
-    @pl.when(meet != s)
-    def _():
-        wait_bytes(feat.at[0], send_sem.at[2])
-
-    others = PEERS - (row_leads[1] - row_leads[0]) - jnp.where(lead, 0, 1)
-
-    @pl.loop(0, others)
-    def _(k):
-        wait_bytes(own, send_sem.at[3])
-
-    reached = PEERS - jnp.where(lead, 0, 1)
-    for limits in LEADS:
-        reached -= within(e, limits).astype(jnp.int32)
-
-    @pl.loop(0, reached)
-    def _(k):
-        wait_bytes(at, send_sem.at[4])
-
-    wait_bytes(lead_in.at[0, pl.ds(0, 2 * (sum(high - low for low, high in LEADS) - 1))], send_sem.at[5])
-
-    @pl.when(jnp.logical_not(lead))
-    def _():
-        wait_bytes(lead_in.at[0, pl.ds(0, 2)], send_sem.at[5])
 
 
 def shards(hidden, out_grad, lengths, left_signs, left_index, right_signs):

time: 27.6 us -> 27.1 us (0.982)
  the two profiles are of different devices: /device:TPU:64 before, /device:TPU:6 now
where the time goes in v7:
time: 27.1 us; the launch traced here: 27 us
  Pallas kernels  26 us (96%)
  local copies, waits for them, and re-layouts  0.97 us (4%)
    pallas_call x1, Pallas kernels, shards(): pl.pallas_call(functools.partial(exchange, blocks), out_shape=pltpu.VMEM(...  26 us
    unnamed x1, local copies, waits for them, and re-layouts  0.97 us

profile of v7, /device:TPU:6, one launch (start us, length us, event | category | flops | bytes accessed | tf_op | source)
XLA Modules:
  0.0 27.0 jit_solution(680561071829984541)
XLA Ops:
  0.0 26.0 %exchange.1 = f32[512,512]{1,0:T(8,128)S(1)} custom-call(bf16[512,1792]{1,0:T(8,128)(2,1)} %hidden.1, bf16[512,512]{1,0:T(8,128)(2,1)} %out_grad.1, bf16[128,512]{1,0:T(8,128)(2,1)} %right.1, bf16[14,2,16,128]{3,2,1,0:T(8,128)(2,1)} %signs.1, s32[2,14]{1,0:T(2,128)} %bitcast.1, s32[4]{0:T(128)} %lengths.1), custom_call_target="tpu_custom_call" | custom-call | tf_op jit(solution)/shard_map/exchange/pallas_call | solution.py:384
  26.0 1.0 %copy.8 = f32[512,512]{1,0:T(8,128)} copy(f32[512,512]{1,0:T(8,128)S(1)} %exchange.1) | data formatting | bytes 2097152

commit v8 on v7

--- a/solution.py
+++ b/solution.py
@@ -18,7 +18,7 @@
 EX_DEV = 4
 PEERS = 16
 ZS = 8
-Z_ORDER = (4, 3, 5, 2, 6, 1, 7)
+Z_ORDER = (4, 5, 3, 6, 2, 7, 1)
 Y_ORDER = (2, 3, 1, 0)
 LEADS = ((1, 3), (0, 1), (0, 1), (0, 0), (0, 1))
 X_ORDER = (2, 1, 3, 0)
@@ -242,10 +242,6 @@
                             to,
                         ).start()
 
-    @pl.when(e >= PEERS // 2)
-    def _():
-        to_leads((0,))
-
     meet = y * EX_DEV + lax.rem(e, EX_DEV)
     spot = c_in.at[x, lax.div(e, EX_DEV)]
 
@@ -253,6 +249,10 @@
         remote(feat.at[to], spot, send_sem.at[2], recv_sem.at[2], meet, to).start()
 
     pl.loop(0, e)(give)
+
+    @pl.when(e >= PEERS // 2)
+    def _():
+        to_leads((0,))
 
     @pl.loop(1, PEERS)
     def _(i):

time: 27.1 us -> 27 us (level)
  the two profiles are of different devices: /device:TPU:6 before, /device:TPU:33 now
where the time goes in v8:
time: 27 us; the launch traced here: 26.9 us
  Pallas kernels  25.9 us (96%)
  local copies, waits for them, and re-layouts  0.97 us (4%)
    pallas_call x1, Pallas kernels, shards(): pl.pallas_call(functools.partial(exchange, blocks), out_shape=pltpu.VMEM(...  25.9 us
    unnamed x1, local copies, waits for them, and re-layouts  0.97 us

profile of v8, /device:TPU:33, one launch (start us, length us, event | category | flops | bytes accessed | tf_op | source)
XLA Modules:
  0.0 26.9 jit_solution(9172622276093556353)
XLA Ops:
  0.0 25.9 %exchange.1 = f32[512,512]{1,0:T(8,128)S(1)} custom-call(bf16[512,1792]{1,0:T(8,128)(2,1)} %hidden.1, bf16[512,512]{1,0:T(8,128)(2,1)} %out_grad.1, bf16[128,512]{1,0:T(8,128)(2,1)} %right.1, bf16[14,2,16,128]{3,2,1,0:T(8,128)(2,1)} %signs.1, s32[2,14]{1,0:T(2,128)} %bitcast.1, s32[4]{0:T(128)} %lengths.1), custom_call_target="tpu_custom_call" | custom-call | tf_op jit(solution)/shard_map/exchange/pallas_call | solution.py:384
  25.9 1.0 %copy.8 = f32[512,512]{1,0:T(8,128)} copy(f32[512,512]{1,0:T(8,128)S(1)} %exchange.1) | data formatting | bytes 2097152
